TPU v7x, 512 devices: a whole 4x4x16 slice. The times are simulated.
512 devices in a mesh: fsdp: 16 (over y, z_hi, core), seq: 32 (over x, z_lo).
Axes of the slice: x: 4, y: 4, z: 16 (z_hi: 2, z_lo: 8; z = z_hi * 8 + z_lo), core: 2. Of those that a mesh axis runs over, the one named last changes fastest.
Arguments:
- query_raw: bfloat16 [16, 4096, 4096], P('fsdp', 'seq'), may hold values from -450 to 450, as said below
- out_cotangent: bfloat16 [16, 4096, 4096], P('fsdp', 'seq'), may hold values from -72 to 72, as said below
- text_keys: bfloat16 [16, 512, 4096], P('fsdp', 'seq'), may hold values from -450 to 450, as said below
- text_values: bfloat16 [16, 512, 4096], P('fsdp', 'seq'), may hold values from -24 to 24
- text_lengths: int32 [16], P('fsdp'), may hold values from 256 to 512
- gain_query: float32 [4096], P('fsdp'), may hold values from 0.1 to 1.9
- gain_key: float32 [4096], P('fsdp'), may hold values from 0.1 to 1.9
Outputs:
- attention_out: bfloat16 [16, 4096, 4096], P('fsdp', 'seq')
- query_grad: bfloat16 [16, 4096, 4096], P('fsdp', 'seq')
- gain_grad: float32 [4096], P('fsdp')
Inputs may be any that keep to these rules, and one draw needn't show every extreme that they name: `query_raw`: finite values. `text_keys`: finite values. `out_cotangent`: finite values.
All inputs are finite; a program needn't handle non-finite values.
Results may differ from a plain program's by a relative error of at most 0.034.
Values may be sent and summed in bfloat16 or wider, within the bound.
A program may use at most 64 MiB of HBM per device.

v0:
```python
import math

import jax
import jax.numpy as jnp
from jax import lax
from jax.sharding import PartitionSpec as P

HEADS = 32


epsilon = 1e-06
masked_value = -1e30


def unit_rows(entries):
    inverse = lax.rsqrt(jnp.mean(entries * entries, axis=-1, keepdims=True) + epsilon)
    return (inverse, entries * inverse)


def block_attention(queries, key_rows, value_rows, cotangent, usable):
    scores = jnp.einsum("thd,jhd->htj", queries, key_rows, preferred_element_type=jnp.float32)
    scores = jnp.where(usable[None, None, :], scores, masked_value)
    row_max = jnp.max(scores, axis=-1, keepdims=True)
    exponent_terms = jnp.exp(scores - row_max)
    softmax = exponent_terms / jnp.sum(exponent_terms, axis=-1, keepdims=True)
    outputs = jnp.einsum(
        "htj,jhd->thd", softmax.astype(jnp.bfloat16), value_rows, preferred_element_type=jnp.float32
    ).astype(jnp.bfloat16)
    row_delta = jnp.sum(cotangent.astype(jnp.float32) * outputs.astype(jnp.float32), axis=-1)
    prob_grad = jnp.einsum(
        "thd,jhd->htj", cotangent, value_rows, preferred_element_type=jnp.float32
    )
    score_grad = (softmax * (prob_grad - jnp.transpose(row_delta)[:, :, None])).astype(jnp.bfloat16)
    query_grad = jnp.einsum(
        "htj,jhd->thd", score_grad, key_rows, preferred_element_type=jnp.float32
    ).astype(jnp.bfloat16)
    return (outputs, query_grad)


def attend(queries, key_rows, value_rows, cotangent, length):
    row_total, head_total, head_size = queries.shape
    key_count = key_rows.shape[0]
    row_block = min(row_total, 512)
    head_block = math.gcd(head_total, max(1, 1024 // row_block))
    head_groups = head_total // head_block
    usable = jnp.arange(key_count) < length

    def split_heads(blocks, count_rows):
        return jnp.moveaxis(blocks.reshape(count_rows, head_groups, head_block, head_size), 1, 0)

    def merge_heads(blocks):
        return jnp.moveaxis(blocks, 0, 1).reshape(row_block, head_total, head_size)

    key_groups = split_heads(key_rows, key_count)
    value_groups = split_heads(value_rows, key_count)

    def head_step(bundle):
        return block_attention(bundle[0], bundle[1], bundle[2], bundle[3], usable)

    def row_step(bundle):
        outputs, gradients = lax.map(
            head_step,
            (
                split_heads(bundle[0], row_block),
                key_groups,
                value_groups,
                split_heads(bundle[1], row_block),
            ),
        )
        return (merge_heads(outputs), merge_heads(gradients))

    block_shape = (row_total // row_block, row_block, head_total, head_size)
    outputs, gradients = lax.map(
        row_step, (queries.reshape(block_shape), cotangent.reshape(block_shape))
    )
    return (
        outputs.reshape(row_total, head_total, head_size),
        gradients.reshape(row_total, head_total, head_size),
    )


def on_device(query_raw, out_cotangent, text_keys, text_values, text_lengths, gain_query, gain_key):
    full_query_gain, full_key_gain = (
        lax.all_gather(gain_query, "fsdp", axis=0, tiled=True),
        lax.all_gather(gain_key, "fsdp", axis=0, tiled=True),
    )
    width_total = query_raw.shape[2]
    head_size = width_total // HEADS
    score_scale = head_size ** (-0.5)
    inverse, q_unit = unit_rows(query_raw[0].astype(jnp.float32))
    q_norm = (q_unit * full_query_gain * score_scale).astype(jnp.bfloat16)
    k_unit = unit_rows(text_keys[0].astype(jnp.float32))[1]
    k_norm = (k_unit * full_key_gain).astype(jnp.bfloat16)
    length = text_lengths[0]
    q_heads, g_heads, k_heads, v_heads = (
        lax.all_to_all(q_norm, "seq", split_axis=1, concat_axis=0, tiled=True),
        lax.all_to_all(out_cotangent[0], "seq", split_axis=1, concat_axis=0, tiled=True),
        lax.all_to_all(k_norm, "seq", split_axis=1, concat_axis=0, tiled=True),
        lax.all_to_all(text_values[0], "seq", split_axis=1, concat_axis=0, tiled=True),
    )
    local_heads = q_heads.shape[1] // head_size
    outputs, gradients = attend(
        q_heads.reshape(-1, local_heads, head_size),
        k_heads.reshape(-1, local_heads, head_size),
        v_heads.reshape(-1, local_heads, head_size),
        g_heads.reshape(-1, local_heads, head_size),
        length,
    )
    attention, dq_norm = (
        lax.all_to_all(
            outputs.reshape(-1, local_heads * head_size),
            "seq",
            split_axis=0,
            concat_axis=1,
            tiled=True,
        ),
        lax.all_to_all(
            gradients.reshape(-1, local_heads * head_size),
            "seq",
            split_axis=0,
            concat_axis=1,
            tiled=True,
        ),
    )
    dq_float = dq_norm.astype(jnp.float32)
    dq_unit = dq_float * full_query_gain * score_scale
    query_grad = (
        inverse * (dq_unit - q_unit * jnp.mean(dq_unit * q_unit, axis=-1, keepdims=True))
    ).astype(jnp.bfloat16)
    gain_part = jnp.sum(dq_float * q_unit, axis=0) * score_scale
    summed_all = lax.psum(gain_part, ("fsdp", "seq"))
    share_width = summed_all.shape[0] // lax.axis_size("fsdp")
    gain_grad = lax.dynamic_slice_in_dim(
        summed_all, lax.axis_index("fsdp") * share_width, share_width
    )
    return (attention[None], query_grad[None], gain_grad)


def solution(mesh):
    in_specs = (
        P("fsdp", "seq", None),
        P("fsdp", "seq", None),
        P("fsdp", "seq", None),
        P("fsdp", "seq", None),
        P("fsdp"),
        P("fsdp"),
        P("fsdp"),
    )
    out_specs = (P("fsdp", "seq", None), P("fsdp", "seq", None), P("fsdp"))
    return jax.shard_map(
        on_device, mesh=mesh, in_specs=in_specs, out_specs=out_specs, check_vma=False
    )
```

profile of v0, /device:TPU:1, one launch (start us, length us, event | category | flops | bytes accessed | tf_op | source)
XLA Modules:
  0.0 480.8 jit_solution(4703551951122783829)
XLA Ops:
  2.8 51.2 %all-gather.1 = f32[16,1,256]{2,1,0:T(1,128)S(1)} all-gather(f32[1,1,256]{2,1,0:T(1,128)} %bitcast.148), channel_id=1, replica_groups=mesh['fsdp'=16,'seq'=32] {'fsdp'}, dimensions={0}, use_global_device_ids=true | all-gather | bytes 17408 | tf_op jit(solution)/shard_map/all_gather | solution.py:85
  54.8 7.6 %all-to-all-start.1 = ((bf16[16,32,128]{2,0,1:T(8,128)(2,1)}), bf16[16,32,128]{2,0,1:T(8,128)(2,1)S(1)}, u32[]{:S(2)}, u32[]{:S(2)}) async-start(bf16[16,32,128]{2,0,1:T(8,128)(2,1)} %copy.51), calls=%async_computation.1 | async-start | bytes 262144 | tf_op jit(solution)/shard_map/all_to_all | solution.py:98
  63.6 36.0 %all-gather = f32[16,1,256]{2,1,0:T(1,128)S(1)} all-gather(f32[1,1,256]{2,1,0:T(1,128)S(1)} %bitcast.149), channel_id=1, replica_groups=mesh['fsdp'=16,'seq'=32] {'fsdp'}, dimensions={0}, use_global_device_ids=true | all-gather | bytes 17408 | tf_op jit(solution)/shard_map/all_gather | solution.py:84
  99.7 1.9 multiply_convert_fusion
  101.6 12.3 %all-to-all-start = ((bf16[128,32,128]{0,2,1:T(8,128)(2,1)}), bf16[128,32,128]{0,2,1:T(8,128)(2,1)S(1)}, u32[]{:S(2)}, u32[]{:S(2)}) async-start(bf16[128,32,128]{0,2,1:T(8,128)(2,1)} %get-tuple-element.158), calls=%async_computation | async-start | bytes 2097152 | tf_op jit(solution)/shard_map/all_to_all | solution.py:96
  113.9 1.3 copy.53
  115.2 49.2 %all-to-all-done = bf16[128,32,128]{0,2,1:T(8,128)(2,1)S(1)} async-done(((bf16[128,32,128]{0,2,1:T(8,128)(2,1)}), bf16[128,32,128]{0,2,1:T(8,128)(2,1)S(1)}, u32[]{:S(2)}, u32[]{:S(2)}) %all-to-all-start) | async-done | bytes 1048608 | tf_op jit(solution)/shard_map/all_to_all | solution.py:96
  164.4 6.7 %all-to-all-start.3 = ((bf16[128,32,128]{0,2,1:T(8,128)(2,1)}), bf16[128,32,128]{0,2,1:T(8,128)(2,1)S(1)}, u32[]{:S(2)}, u32[]{:S(2)}) async-start(bf16[128,32,128]{0,2,1:T(8,128)(2,1)} %bitcast.134), calls=%async_computation.3 | async-start | bytes 2097152 | tf_op jit(solution)/shard_map/all_to_all | solution.py:97
  171.9 49.6 %all-to-all-done.3 = bf16[128,32,128]{0,2,1:T(8,128)(2,1)S(1)} async-done(((bf16[128,32,128]{0,2,1:T(8,128)(2,1)}), bf16[128,32,128]{0,2,1:T(8,128)(2,1)S(1)}, u32[]{:S(2)}, u32[]{:S(2)}) %all-to-all-start.3) | async-done | bytes 1048608 | tf_op jit(solution)/shard_map/all_to_all | solution.py:97
  221.6 6.3 %all-to-all-start.2 = ((bf16[16,32,128]{2,0,1:T(8,128)(2,1)}), bf16[16,32,128]{2,0,1:T(8,128)(2,1)S(1)}, u32[]{:S(2)}, u32[]{:S(2)}) async-start(bf16[16,32,128]{2,0,1:T(8,128)(2,1)} %copy.52), calls=%async_computation.2 | async-start | bytes 262144 | tf_op jit(solution)/shard_map/all_to_all | solution.py:99
  227.8 1.3 copy.50
  229.2 1.3 copy.54
  230.5 9.1 %all-to-all-done.2 = bf16[16,32,128]{2,0,1:T(8,128)(2,1)S(1)} async-done(((bf16[16,32,128]{2,0,1:T(8,128)(2,1)}), bf16[16,32,128]{2,0,1:T(8,128)(2,1)S(1)}, u32[]{:S(2)}, u32[]{:S(2)}) %all-to-all-start.2) | async-done | bytes 131104 | tf_op jit(solution)/shard_map/all_to_all | solution.py:99
  239.6 52.5 %while.13 = (s32[]{:T(128)}, bf16[8,512,1,128]{3,1,0,2:T(8,128)(2,1)}, bf16[8,512,1,128]{3,1,2,0:T(8,128)(2,1)}, bf16[8,512,1,128]{3,1,2,0:T(8,128)(2,1)}, bf16[...) while((s32[]{:T(128)}, ...), condition=%wide.region_6.7_spmd.clone, body=%wide.region_2.6_spmd.clone.sunk | while | flops 271973376 | bytes 6444133 | solution.py:73
  243.1 2.3 fusion.50
  249.6 2.3 fusion.50
  256.2 2.3 fusion.50
  262.8 2.3 fusion.50
  266.5 1.2 fusion.47
  269.3 2.3 fusion.50
  273.1 1.2 fusion.47
  275.9 2.3 fusion.50
  282.4 2.3 fusion.50
  289.0 2.3 fusion.50
  292.1 1.6 copy.60
  293.7 57.0 %all_to_all.87 = bf16[32,128,128]{1,2,0:T(8,128)(2,1)S(1)} all-to-all(bf16[32,128,128]{1,2,0:T(8,128)(2,1)S(1)} %copy.60), channel_id=1, replica_groups=mesh['fsdp'=16,'seq'=32] {'seq'}, dimensions={0} | all-to-all | bytes 2097152 | tf_op jit(solution)/shard_map/all_to_all | solution.py:117
  350.7 6.1 %all-to-all-start.4 = ((bf16[32,128,128]{2,1,0:T(8,128)(2,1)}), bf16[32,128,128]{2,1,0:T(8,128)(2,1)S(1)}, u32[]{:S(2)}, u32[]{:S(2)}) async-start(bf16[32,128,128]{2,1,0:T(8,128)(2,1)} %bitcast.139), calls=%async_computation.4 | async-start | bytes 2097152 | tf_op jit(solution)/shard_map/all_to_all | solution.py:110
  357.1 1.3 copy-done
  358.4 1.4 fusion.29
  360.5 1.3 copy.62
  361.8 116.4 %psum.7 = f32[4096]{0:T(1024)S(1)} all-reduce(f32[4096]{0:T(1024)S(1)} %multiply_bitcast_fusion), channel_id=1, replica_groups=mesh['fsdp'=16,'seq'=32] {'fsdp','seq'}, use_global_device_ids=true, to_apply=%region_9.10 | all-reduce | flops 4096 | bytes 32768 | tf_op jit(solution)/shard_map/psum | solution.py:131
  478.9 1.3 copy.61
  (92 shorter events, 38.7 us)
Async XLA Ops:
  0.6 61.8 %copy-start.1 = (bf16[1,128,4096]{2,1,0:T(8,128)(2,1)S(1)}, bf16[1,128,4096]{2,1,0:T(8,128)(2,1)}, u32[]{:S(2)}) copy-start(bf16[1,128,4096]{2,1,0:T(8,128)(2,1)} %param.9) | copy-start | bytes 3145732
  2.8 60.9 %copy-start.4 = (f32[256]{0:T(256)S(1)}, f32[256]{0:T(256)}, u32[]{:S(2)}) copy-start(f32[256]{0:T(256)} %param.14) | copy-start | bytes 3076
  54.8 46.8 %all-to-all-start.1 = ((bf16[16,32,128]{2,0,1:T(8,128)(2,1)}), bf16[16,32,128]{2,0,1:T(8,128)(2,1)S(1)}, u32[]{:S(2)}, u32[]{:S(2)}) async-start(bf16[16,32,128]{2,0,1:T(8,128)(2,1)} %copy.51), calls=%async_computation.1 | async-start | bytes 262144 | tf_op jit(solution)/shard_map/all_to_all | solution.py:98
  101.6 12.3 %copy-start.2 = (bf16[1,128,4096]{2,1,0:T(8,128)(2,1)S(1)}, bf16[1,128,4096]{2,1,0:T(8,128)(2,1)}, u32[]{:S(2)}) copy-start(bf16[1,128,4096]{2,1,0:T(8,128)(2,1)} %param.10) | copy-start | bytes 3145732
  101.6 62.8 %all-to-all-start = ((bf16[128,32,128]{0,2,1:T(8,128)(2,1)}), bf16[128,32,128]{0,2,1:T(8,128)(2,1)S(1)}, u32[]{:S(2)}, u32[]{:S(2)}) async-start(bf16[128,32,128]{0,2,1:T(8,128)(2,1)} %get-tuple-element.158), calls=%async_computation | async-start | bytes 2097152 | tf_op jit(solution)/shard_map/all_to_all | solution.py:96
  113.9 57.3 %copy-start.3 = (bf16[1,16,4096]{2,1,0:T(8,128)(2,1)S(1)}, bf16[1,16,4096]{2,1,0:T(8,128)(2,1)}, u32[]{:S(2)}) copy-start(bf16[1,16,4096]{2,1,0:T(8,128)(2,1)} %param.12) | copy-start | bytes 393220
  164.4 57.1 %all-to-all-start.3 = ((bf16[128,32,128]{0,2,1:T(8,128)(2,1)}), bf16[128,32,128]{0,2,1:T(8,128)(2,1)S(1)}, u32[]{:S(2)}, u32[]{:S(2)}) async-start(bf16[128,32,128]{0,2,1:T(8,128)(2,1)} %bitcast.134), calls=%async_computation.3 | async-start | bytes 2097152 | tf_op jit(solution)/shard_map/all_to_all | solution.py:97
  221.6 18.1 %all-to-all-start.2 = ((bf16[16,32,128]{2,0,1:T(8,128)(2,1)}), bf16[16,32,128]{2,0,1:T(8,128)(2,1)S(1)}, u32[]{:S(2)}, u32[]{:S(2)}) async-start(bf16[16,32,128]{2,0,1:T(8,128)(2,1)} %copy.52), calls=%async_computation.2 | async-start | bytes 262144 | tf_op jit(solution)/shard_map/all_to_all | solution.py:99
  350.7 127.5 %all-to-all-start.4 = ((bf16[32,128,128]{2,1,0:T(8,128)(2,1)}), bf16[32,128,128]{2,1,0:T(8,128)(2,1)S(1)}, u32[]{:S(2)}, u32[]{:S(2)}) async-start(bf16[32,128,128]{2,1,0:T(8,128)(2,1)} %bitcast.139), calls=%async_computation.4 | async-start | bytes 2097152 | tf_op jit(solution)/shard_map/all_to_all | solution.py:110
  356.8 1.6 copy-start
where the time goes:
time: 482 us; the launch traced here: 481 us
  blocking collectives  261 us (54%)
  waiting for transfers between devices  108 us (22%)
  starting transfers between devices  38.9 us (8%)
  matrix products  30.9 us (6%)
  local copies, waits for them, and re-layouts  27.5 us (6%)
  other arithmetic  13.8 us (3%)
    psum x1, blocking collectives, on_device(): summed_all = lax.psum(gain_part, ('fsdp', 'seq'))  116 us
    all_to_all x1, blocking collectives, on_device(): lax.all_to_all(gradients.reshape(-1, local_heads * head_size), 'seq', spl...  57 us
    all_gather x1, blocking collectives, on_device(): lax.all_gather(gain_key, 'fsdp', axis=0, tiled=True)  51.2 us
    all_to_all x1, waiting for transfers between devices, on_device(): lax.all_to_all(out_cotangent[0], 'seq', split_axis=1, concat_axis=0, tile...  49.6 us
    all_to_all x1, waiting for transfers between devices, on_device(): lax.all_to_all(q_norm, 'seq', split_axis=1, concat_axis=0, tiled=True)  49.2 us
    all_gather x1, blocking collectives, on_device(): lax.all_gather(gain_query, 'fsdp', axis=0, tiled=True)  36 us
    dot_general x8, matrix products, block_attention(): jnp.einsum('htj,jhd->thd', score_grad, key_rows, preferred_element_type=j...  18.3 us
    all_to_all x1, starting transfers between devices, on_device(): lax.all_to_all(q_norm, 'seq', split_axis=1, concat_axis=0, tiled=True)  12.3 us
  transfers between devices with their start and end apart: 5, of which 3 were waited for; matrix products, arithmetic and copies ran while one was open for 2% of the time, Pallas kernels for 0%

commit v1 on v0

v1 whole, which is shorter than its diff:
```python
import functools

import jax
import jax.numpy as jnp
from jax import lax
from jax.experimental import pallas as pl
from jax.experimental.pallas import tpu as pltpu
from jax.sharding import PartitionSpec as P

MESH = pl.DeviceIdType.MESH
DH = 128
NX = 4
NL = 4
EPS = 1e-6
LOG2E = 1.4426950408889634
MASKED = -1e30
VMEM_LIMIT = 61 * 1024 * 1024
F32 = jnp.float32
BF16 = jnp.bfloat16


def attention_kernel(
    dims,
    len_ref,
    q_hbm,
    do_hbm,
    k_hbm,
    v_hbm,
    gq_ref,
    gk_ref,
    att,
    grad,
    gg_ref,
    kv,
    kv_send,
    kraw,
    vraw,
    q,
    qin,
    o_send,
    dqin,
    inv_row,
    inv,
    rowacc,
    gains,
    part,
    row_part,
    sum_y,
    sum_l,
    sum_x,
    sum_z,
    load_sem,
    own_sem,
    kvx_sem,
    z_recv,
    zu_send,
    zd_send,
    in_send,
    in_recv,
    o_send_sem,
    o_recv,
    dq_send_sem,
    dq_recv,
    inv_sem,
    gain_sem,
    sum_sem,
):
    nz, nf, heads, rows, text = dims
    ny = nf // NL
    own_heads = heads // NX
    depth = text // (NX * nz)
    groups = own_heads
    wx = own_heads * DH
    dev_heads = heads // nf
    f = lax.axis_index("fsdp")
    s = lax.axis_index("seq")
    x = s // nz
    z = s % nz
    y = f // NL
    low = f % NL

    def at_x(i):
        return (f, ((x + i) % NX) * nz + z)

    def at_z(i):
        return (f, x * nz + (z + i) % nz)

    def at_y(i):
        return (((y + i) % ny) * NL + low, s)

    def at_low(i):
        return (y * NL + (low + i) % NL, s)

    peers = (
        [at_x(i) for i in range(1, NX)]
        + [at_z(i) for i in range(1, nz)]
        + [at_y(i) for i in range(1, ny)]
        + [at_low(i) for i in range(1, NL)]
    )

    def remote(src, dst, send, recv, target):
        return pltpu.make_async_remote_copy(
            src_ref=src,
            dst_ref=dst,
            send_sem=send,
            recv_sem=recv,
            device_id=target,
            device_id_type=MESH,
        )

    load_k = pltpu.make_async_copy(k_hbm, kraw, load_sem.at[0])
    load_v = pltpu.make_async_copy(v_hbm, vraw, load_sem.at[1])
    load_q = pltpu.make_async_copy(q_hbm, q, load_sem.at[2])
    for load in (load_k, load_v, load_q):
        load.start()

    barrier = pltpu.get_barrier_semaphore()
    for peer in peers:
        pl.semaphore_signal(barrier, inc=1, device_id=peer, device_id_type=MESH)

    def columns(head):
        return pl.ds(pl.multiple_of(head * DH, DH), DH)

    @pl.loop(0, groups)
    def _(g):
        cols = columns(x * groups + g)
        pltpu.make_async_copy(q_hbm.at[:, cols], qin.at[g, x, 0], own_sem).start()
        pltpu.make_async_copy(do_hbm.at[:, cols], qin.at[g, x, 1], own_sem).start()

    for i in range(dev_heads):
        gains[dev_heads * f + i, 0:1] = gq_ref[i]
        gains[dev_heads * f + i, 1:2] = gk_ref[i]

    load_k.wait()
    load_v.wait()
    k32 = kraw[...].astype(F32)
    k_unit = k32 * lax.rsqrt(jnp.mean(k32 * k32, axis=-1, keepdims=True) + EPS)
    k_unit = k_unit.astype(BF16)
    for h in range(heads):
        kv_send[h // groups, h % groups, 0] = k_unit[:, h * DH : (h + 1) * DH]
        kv_send[h // groups, h % groups, 1] = vraw[:, h * DH : (h + 1) * DH]
    kv[:, z, x] = kv_send[x]

    load_q.wait()
    q32 = q[...].astype(F32)
    inv_col = lax.rsqrt(jnp.mean(q32 * q32, axis=-1, keepdims=True) + EPS)
    inv_wide = jnp.broadcast_to(inv_col, (rows, DH))
    inv[x] = inv_wide
    inv_row[x] = jnp.transpose(inv_wide)[0:1, :]
    rowacc[...] = jnp.zeros_like(rowacc)

    pl.semaphore_wait(barrier, len(peers))

    def kvx_copy(i):
        return remote(
            kv_send.at[(x + i) % NX], kv.at[:, z, x], kvx_sem.at[0], kvx_sem.at[1], at_x(i)
        )

    def inv_copy(i):
        return remote(inv_row.at[x], inv_row.at[x], inv_sem.at[0], inv_sem.at[1], at_x(i))

    def in_copies(g, i):
        cols = columns(((x + i) % NX) * groups + g)
        return (
            remote(q_hbm.at[:, cols], qin.at[g, x, 0], in_send, in_recv.at[g, x], at_x(i)),
            remote(do_hbm.at[:, cols], qin.at[g, x, 1], in_send, in_recv.at[g, x], at_x(i)),
        )

    def out_copies(g, i):
        head = x * groups + g
        to = (x + i) % NX
        return (
            remote(o_send.at[g, to, 0], att.at[:, columns(head)], o_send_sem, o_recv, at_x(i)),
            remote(o_send.at[g, to, 1], dqin.at[head], dq_send_sem, dq_recv.at[g], at_x(i)),
        )

    def z_copy(g, zz, up):
        chunk = kv.at[g, zz]
        send = zu_send if up else zd_send
        return remote(
            chunk, chunk, send.at[zz], z_recv.at[g, zz], at_z(1) if up else at_z(nz - 1)
        )

    def settle_recv(ref, sem):
        remote(ref, ref, sem, sem, at_x(1)).wait_recv()

    def settle_send(ref, sem):
        remote(ref, ref, sem, sem, at_x(1)).wait_send()

    for i in range(1, NX):
        kvx_copy(i).start()

    def in_sends(g):
        for i in range(1, NX):
            for copy in in_copies(g, i):
                copy.start()

    in_sends(0)
    for i in range(1, NX):
        inv_copy(i).start()

    block = gains.at[pl.ds(dev_heads * f, dev_heads)]
    for i in range(1, NL):
        remote(block, block, gain_sem.at[0], gain_sem.at[1], at_low(i)).start()

    index = lax.broadcasted_iota(jnp.int32, (1, text), 1)
    chunk_rows = NX * depth
    token = ((index // depth) % NX * nz + index // chunk_rows) * depth + index % depth
    bias = jnp.where(token < len_ref[0], 0.0, MASKED).astype(F32)
    scale = DH**-0.5
    nt = (((1,), (1,)), ((), ()))

    def compute(g):
        head = x * groups + g
        gain_q = gains[head, 0:1]
        gain_k = gains[head, 1:2]
        factor = gain_q * gain_k * (scale * LOG2E)
        keys = kv[g, :, :, 0].reshape(text, DH)
        values = kv[g, :, :, 1].reshape(text, DH)
        for i in (1, 2, 3, 0):
            source = (x + i) % NX
            q_low = (qin[g, source, 0].astype(F32) * inv[source] * factor).astype(BF16)
            cot = qin[g, source, 1]
            sc = lax.dot_general(q_low, keys, nt, preferred_element_type=F32) + bias
            e = jnp.exp2(sc - jnp.max(sc, axis=-1, keepdims=True))
            inv_sum = 1.0 / jnp.sum(e, axis=-1, keepdims=True)
            o = jnp.dot(e.astype(BF16), values, preferred_element_type=F32) * inv_sum
            o_low = o.astype(BF16)
            delta = jnp.sum(cot.astype(F32) * o_low.astype(F32), axis=-1, keepdims=True)
            dp = lax.dot_general(cot, values, nt, preferred_element_type=F32)
            ds = (e * (dp - delta)).astype(BF16)
            dq = jnp.dot(ds, keys, preferred_element_type=F32) * inv_sum * gain_k
            if i == 0:
                att[:, columns(head)] = o_low
                dqin[head] = dq.astype(BF16)
            else:
                o_send[g, source, 0] = o_low
                o_send[g, source, 1] = dq.astype(BF16)
                for copy in out_copies(g, i):
                    copy.start()

    def post(g):
        settle_recv(dqin.at[pl.ds(0, NX - 1)], dq_recv.at[g])
        for xx in range(NX):
            head = xx * groups + g
            q_unit = q[:, columns(head)].astype(F32) * inv[x]
            product = dqin[head].astype(F32) * q_unit
            rowacc[...] += product * (gains[head, 0:1] * scale)
            part[head] = jnp.sum(product, axis=0, keepdims=True) * scale

    last = nz - 1

    def step(n, carry):
        @pl.when(n == 0)
        def _():
            settle_recv(kv.at[:, z, 0 : NX - 1], kvx_sem.at[1])

        @pl.when(n < groups)
        def _():
            @pl.when(z < last)
            def _():
                z_copy(n, z, True).start()

            @pl.when(z > 0)
            def _():
                z_copy(n, z, False).start()

        @pl.loop(1, nz)
        def _(d):
            g = n - d
            live = jnp.logical_and(g >= 0, g < groups)

            @pl.when(jnp.logical_and(live, z - d >= 0))
            def _():
                z_copy(g, z - d, True).wait_recv()

                @pl.when(z < last)
                def _():
                    z_copy(g, z - d, True).start()

            @pl.when(jnp.logical_and(live, z + d < nz))
            def _():
                z_copy(g, z + d, False).wait_recv()

                @pl.when(z > 0)
                def _():
                    z_copy(g, z + d, False).start()

        @pl.when(n + 1 < groups)
        def _():
            in_sends(n + 1)

        @pl.when(n == min(1, last - 1))
        def _():
            settle_recv(gains.at[pl.ds(0, (NL - 1) * dev_heads)], gain_sem.at[1])
            row = gains.at[pl.ds(y * NL * dev_heads, NL * dev_heads)]
            for i in range(1, ny):
                remote(row, row, gain_sem.at[2], gain_sem.at[3], at_y(i)).start()

        @pl.when(n == min(2, last - 1))
        def _():
            if ny > 1:
                settle_recv(gains.at[pl.ds(0, (ny - 1) * NL * dev_heads)], gain_sem.at[3])
            settle_recv(inv_row.at[pl.ds(0, NX - 1)], inv_sem.at[1])
            for i in range(1, NX):
                source = (x + i) % NX
                wide = jnp.broadcast_to(inv_row[source], (DH, rows))
                inv[source] = jnp.transpose(wide)[:, 0:DH]
            pltpu.make_async_copy(qin.at[:, x], qin.at[:, x], own_sem).wait()

        done = n - last

        @pl.when(jnp.logical_and(done >= 0, done < groups))
        def _():
            for i in range(1, NX):
                source = (x + i) % NX
                settle_recv(qin.at[done, source], in_recv.at[done, source])
            compute(done)

        returned = done - 2

        @pl.when(jnp.logical_and(returned >= 0, returned < groups))
        def _():
            post(returned)

        return carry

    lax.fori_loop(0, groups + last + 2, step, 0)

    def final(first, count):
        @pl.loop(first, first + count)
        def _(head):
            dq_unit = dqin[head].astype(F32) * (gains[head, 0:1] * scale)
            result = inv[x] * dq_unit - q[:, columns(head)].astype(F32) * slope
            grad[:, columns(head)] = result.astype(BF16)

    for i in range(1, ny):
        to = (y + i) % ny
        remote(
            part.at[pl.ds(to * NL * dev_heads, NL * dev_heads)],
            sum_y.at[y],
            sum_sem.at[0],
            sum_sem.at[1],
            at_y(i),
        ).start()
    sum_y[y] = part[pl.ds(y * NL * dev_heads, NL * dev_heads)]
    row_mean = jnp.sum(rowacc[...], axis=-1, keepdims=True) * (1.0 / (heads * DH))
    slope = inv[x] * inv[x] * row_mean
    final(0, heads // 4)
    if ny > 1:
        settle_recv(sum_y.at[pl.ds(0, ny - 1)], sum_sem.at[1])
    total = sum_y[0]
    for i in range(1, ny):
        total = total + sum_y[i]
    row_part[...] = total
    for i in range(1, NL):
        to = (low + i) % NL
        remote(
            row_part.at[pl.ds(to * dev_heads, dev_heads)],
            sum_l.at[low],
            sum_sem.at[2],
            sum_sem.at[3],
            at_low(i),
        ).start()
    sum_l[low] = row_part[pl.ds(low * dev_heads, dev_heads)]
    final(heads // 4, heads // 4)
    settle_recv(sum_l.at[pl.ds(0, NL - 1)], sum_sem.at[3])
    total = sum_l[0]
    for i in range(1, NL):
        total = total + sum_l[i]
    sum_x[x] = total
    for i in range(1, NX):
        remote(sum_x.at[x], sum_x.at[x], sum_sem.at[4], sum_sem.at[5], at_x(i)).start()
    final(heads // 2, heads // 4)
    settle_recv(sum_x.at[pl.ds(0, NX - 1)], sum_sem.at[5])
    total = sum_x[0]
    for i in range(1, NX):
        total = total + sum_x[i]
    sum_z[z] = total
    for i in range(1, nz):
        remote(sum_z.at[z], sum_z.at[z], sum_sem.at[6], sum_sem.at[7], at_z(i)).start()
    final(3 * heads // 4, heads // 4)

    settle_recv(att.at[:, 0 : (NX - 1) * wx], o_recv)
    settle_send(kv_send.at[0 : NX - 1], kvx_sem.at[0])
    settle_send(qin.at[:, 0 : NX - 1], in_send)
    settle_send(o_send.at[:, 0 : NX - 1, 0], o_send_sem)
    settle_send(o_send.at[:, 0 : NX - 1, 1], dq_send_sem)
    settle_send(inv_row.at[pl.ds(0, NX - 1)], inv_sem.at[0])
    settle_send(gains.at[pl.ds(0, (NL - 1) * dev_heads)], gain_sem.at[0])
    if ny > 1:
        settle_send(gains.at[pl.ds(0, (ny - 1) * NL * dev_heads)], gain_sem.at[2])

    @pl.loop(0, nz)
    def _(zz):
        @pl.when(jnp.logical_and(z < last, zz <= z))
        def _():
            settle_send(kv.at[:, zz], zu_send.at[zz])

        @pl.when(jnp.logical_and(z > 0, zz >= z))
        def _():
            settle_send(kv.at[:, zz], zd_send.at[zz])

    if ny > 1:
        settle_send(sum_y.at[pl.ds(0, ny - 1)], sum_sem.at[0])
    settle_send(sum_l.at[pl.ds(0, NL - 1)], sum_sem.at[2])
    settle_send(sum_x.at[pl.ds(0, NX - 1)], sum_sem.at[4])
    settle_recv(sum_z.at[pl.ds(0, nz - 1)], sum_sem.at[7])
    total = sum_z[0]
    for i in range(1, nz):
        total = total + sum_z[i]
    gg_ref[...] = total
    settle_send(sum_z.at[pl.ds(0, nz - 1)], sum_sem.at[6])


def on_device(nz, nf, query_raw, out_cotangent, text_keys, text_values, text_lengths, gain_query, gain_key):
    rows, width = query_raw.shape[1:]
    depth = text_keys.shape[1]
    heads = width // DH
    text = depth * NX * nz
    own = heads // NX
    dev_heads = heads // nf
    ny = nf // NL
    dims = (nz, nf, heads, rows, text)
    any_space = pl.BlockSpec(memory_space=pl.ANY)
    vmem = pl.BlockSpec(memory_space=pltpu.VMEM)
    dma = pltpu.SemaphoreType.DMA
    attention, query_grad, gain_grad = pl.pallas_call(
        functools.partial(attention_kernel, dims),
        out_shape=(
            jax.ShapeDtypeStruct((rows, width), BF16),
            jax.ShapeDtypeStruct((rows, width), BF16),
            jax.ShapeDtypeStruct((dev_heads, 1, DH), F32),
        ),
        in_specs=[pl.BlockSpec(memory_space=pltpu.SMEM)] + [any_space] * 4 + [vmem] * 2,
        out_specs=(vmem, vmem, vmem),
        scratch_shapes=[
            pltpu.VMEM((own, nz, NX, 2, depth, DH), BF16),
            pltpu.VMEM((NX, own, 2, depth, DH), BF16),
            pltpu.VMEM((depth, width), BF16),
            pltpu.VMEM((depth, width), BF16),
            pltpu.VMEM((rows, width), BF16),
            pltpu.VMEM((own, NX, 2, rows, DH), BF16),
            pltpu.VMEM((own, NX, 2, rows, DH), BF16),
            pltpu.VMEM((heads, rows, DH), BF16),
            pltpu.VMEM((NX, 1, rows), F32),
            pltpu.VMEM((NX, rows, DH), F32),
            pltpu.VMEM((rows, DH), F32),
            pltpu.VMEM((heads, 2, DH), F32),
            pltpu.VMEM((heads, 1, DH), F32),
            pltpu.VMEM((NL * dev_heads, 1, DH), F32),
            pltpu.VMEM((ny, NL * dev_heads, 1, DH), F32),
            pltpu.VMEM((NL, dev_heads, 1, DH), F32),
            pltpu.VMEM((NX, dev_heads, 1, DH), F32),
            pltpu.VMEM((nz, dev_heads, 1, DH), F32),
            dma((3,)),
            dma,
            dma((2,)),
            dma((own, nz)),
            dma((nz,)),
            dma((nz,)),
            dma,
            dma((own, NX)),
            dma,
            dma,
            dma,
            dma((own,)),
            dma((2,)),
            dma((4,)),
            dma((8,)),
        ],
        compiler_params=pltpu.CompilerParams(
            collective_id=0, has_side_effects=True, vmem_limit_bytes=VMEM_LIMIT
        ),
    )(
        text_lengths,
        query_raw[0],
        out_cotangent[0],
        text_keys[0],
        text_values[0],
        gain_query.reshape(dev_heads, 1, DH),
        gain_key.reshape(dev_heads, 1, DH),
    )
    return attention[None], query_grad[None], gain_grad.reshape(dev_heads * DH)


def solution(mesh):
    nf, ns = mesh.shape["fsdp"], mesh.shape["seq"]
    tokens = P("fsdp", "seq", None)
    return jax.shard_map(
        functools.partial(on_device, ns // NX, nf),
        mesh=mesh,
        in_specs=(tokens, tokens, tokens, tokens, P("fsdp"), P("fsdp"), P("fsdp")),
        out_specs=(tokens, tokens, P("fsdp")),
        check_vma=False,
    )
```

time: 482 us -> 104 us (0.22)
  blocking collectives: 261 us -> 0 us
  waiting for transfers between devices: 108 us -> 0 us
  Pallas kernels: 0 us -> 98.5 us
  starting transfers between devices: 38.9 us -> 0 us
  matrix products: 30.9 us -> 0 us
  local copies, waits for them, and re-layouts: 27.5 us -> 3.92 us
  other arithmetic: 13.8 us -> 0 us
    psum x1 -> x0, blocking collectives: 116 us -> none  [on_device(): summed_all = lax.psum(gain_part, ('fsdp', 'seq'))]
    all_to_all x5 -> x0, waiting for transfers between devices: 108 us -> none  [the longest x1 49.6 us: on_device(): lax.all_to_all(out_cotangent[0], 'seq', split_axis=1, concat_axis=0, tile...]
    pallas_call x0 -> x1, Pallas kernels: none -> 98.5 us  [on_device(): pl.pallas_call(functools.partial(attention_kernel, dims), out_shape=(jax....]
    all_gather x2 -> x0, blocking collectives: 87.2 us -> none  [the longest x1 51.2 us: on_device(): lax.all_gather(gain_key, 'fsdp', axis=0, tiled=True)]
    all_to_all x1 -> x0, blocking collectives: 57 us -> none  [on_device(): lax.all_to_all(gradients.reshape(-1, local_heads * head_size), 'seq', spl...]
    all_to_all x5 -> x0, starting transfers between devices: 38.9 us -> none  [the longest x1 12.3 us: on_device(): lax.all_to_all(q_norm, 'seq', split_axis=1, concat_axis=0, tiled=True)]
    dot_general x24 -> x0, matrix products: 30.9 us -> none  [the longest x8 18.3 us: block_attention(): jnp.einsum('htj,jhd->thd', score_grad, key_rows, preferred_element_type=j...]
    dynamic_slice x17 -> x0, local copies, waits for them, and re-layouts: 8.88 us -> none  [the longest x16 8.24 us: attend(): lax.map(row_step, (queries.reshape(block_shape), cotangent.reshape(block_...]
  transfers between devices with their start and end apart: 5 -> 0, of which waited for: 3 -> 0; matrix products, arithmetic and copies ran while one was open for 2% -> 0% of each run, Pallas kernels for 0% -> 0%
where the time goes in v1:
time: 104 us
  Pallas kernels  98.5 us (95%)
  local copies, waits for them, and re-layouts  3.92 us (4%)
  between operations  1.3 us (1%)
    pallas_call x1, Pallas kernels, on_device(): pl.pallas_call(functools.partial(attention_kernel, dims), out_shape=(jax....  98.5 us
    unnamed x7, local copies, waits for them, and re-layouts  3.92 us

profile of v1, /device:TPU:1, one launch (start us, length us, event | category | flops | bytes accessed | tf_op | source)
XLA Modules:
  0.0 103.7 jit_solution(861086267583461917)
XLA Ops:
  1.3 98.5 %shard_map.94 = (bf16[128,4096]{1,0:T(8,128)(2,1)}, bf16[128,4096]{1,0:T(8,128)(2,1)}, f32[2,1,128]{2,1,0:T(1,128)}) custom-call(s32[1]{0:T(128)S(6)} %copy.13.len_ref, bf16[128,4096]{1,0:T(8,128)(2,1)} %bitcast.9, bf16[128,4096]{1,0:T(8,128)(2,1)} %bitcast.10, bf16[16,4096]{1,0:T(8,128)(2,1)} %bitcast.13, bf16[16,4096]{1,0:T(8,128)(2,1)} %bitcast.14, ...), custom_call_target="tpu_custom_call" | custom-call | tf_op jit(solution)/shard_map/pallas_call | solution.py:428
  99.8 0.0 copy-start
  99.8 2.4 %copy.14 = bf16[1,128,4096]{2,1,0:T(8,128)(2,1)} copy(bf16[1,128,4096]{2,1,0:T(8,128)(2,1)} %bitcast.12) | data formatting | bytes 2097152
  102.1 0.0 copy-done
  102.1 0.0 copy-start.1
  102.2 1.0 copy.15
  103.1 0.0 copy-done.1
  103.1 0.6 copy.16
Async XLA Ops:
  99.8 2.4 %copy-start = (bf16[128,4096]{1,0:T(8,128)(2,1)S(1)}, bf16[128,4096]{1,0:T(8,128)(2,1)}, u32[]{:S(2)}) copy-start(bf16[128,4096]{1,0:T(8,128)(2,1)} %get-tuple-element.7) | copy-start | bytes 3145732
  102.1 1.0 copy-start.1

commit v2 on v1

--- a/solution.py
+++ b/solution.py
@@ -42,12 +42,13 @@
     inv_row,
     inv,
     rowacc,
+    own_gains,
     gains,
     part,
-    row_part,
+    core_part,
+    sum_c,
     sum_y,
-    sum_l,
-    sum_x,
+    z_part,
     sum_z,
     load_sem,
     own_sem,
@@ -85,18 +86,23 @@
     def at_z(i):
         return (f, x * nz + (z + i) % nz)
 
-    def at_y(i):
-        return (((y + i) % ny) * NL + low, s)
-
-    def at_low(i):
-        return (y * NL + (low + i) % NL, s)
-
-    peers = (
-        [at_x(i) for i in range(1, NX)]
-        + [at_z(i) for i in range(1, nz)]
-        + [at_y(i) for i in range(1, ny)]
-        + [at_low(i) for i in range(1, NL)]
-    )
+    core = low % 2
+    half = low // 2
+    other_core = (y * NL + half * 2 + 1 - core, s)
+    other_half = (y * NL + (1 - half) * 2 + core, s)
+    place = half * nz + z
+    places = NL // 2 * nz
+
+    def at_place(i):
+        to = (place + i) % places
+        return (y * NL + to // nz * 2 + core, x * nz + to % nz)
+
+    owner_row = x * NL + low
+
+    barrier = pltpu.get_barrier_semaphore()
+
+    def greet(peer):
+        pl.semaphore_signal(barrier, inc=1, device_id=peer, device_id_type=MESH)
 
     def remote(src, dst, send, recv, target):
         return pltpu.make_async_remote_copy(
@@ -114,22 +120,29 @@
     for load in (load_k, load_v, load_q):
         load.start()
 
-    barrier = pltpu.get_barrier_semaphore()
-    for peer in peers:
-        pl.semaphore_signal(barrier, inc=1, device_id=peer, device_id_type=MESH)
+    @pl.loop(1, places)
+    def _(i):
+        greet(at_place(i))
+
+    for i in range(1, NX):
+        greet(at_x(i))
+    greet(other_core)
+    for i in range(ny):
+        if i == 0:
+
+            @pl.when(x != y)
+            def _():
+                greet((f, y * nz + z))
+
+        else:
+            greet((((y + i) % ny) * NL + low, y * nz + z))
 
     def columns(head):
         return pl.ds(pl.multiple_of(head * DH, DH), DH)
 
-    @pl.loop(0, groups)
-    def _(g):
-        cols = columns(x * groups + g)
-        pltpu.make_async_copy(q_hbm.at[:, cols], qin.at[g, x, 0], own_sem).start()
-        pltpu.make_async_copy(do_hbm.at[:, cols], qin.at[g, x, 1], own_sem).start()
-
     for i in range(dev_heads):
-        gains[dev_heads * f + i, 0:1] = gq_ref[i]
-        gains[dev_heads * f + i, 1:2] = gk_ref[i]
+        own_gains[i, 0:1] = gq_ref[i]
+        own_gains[i, 1:2] = gk_ref[i]
 
     load_k.wait()
     load_v.wait()
@@ -149,7 +162,15 @@
     inv_row[x] = jnp.transpose(inv_wide)[0:1, :]
     rowacc[...] = jnp.zeros_like(rowacc)
 
-    pl.semaphore_wait(barrier, len(peers))
+    near = places - 1 + NX - 1 + 1 + ny - 1
+
+    @pl.when(x == y)
+    def _():
+        pl.semaphore_wait(barrier, near)
+
+    @pl.when(x != y)
+    def _():
+        pl.semaphore_wait(barrier, near + 1)
 
     def kvx_copy(i):
         return remote(
@@ -199,9 +220,30 @@
     for i in range(1, NX):
         inv_copy(i).start()
 
-    block = gains.at[pl.ds(dev_heads * f, dev_heads)]
-    for i in range(1, NL):
-        remote(block, block, gain_sem.at[0], gain_sem.at[1], at_low(i)).start()
+    def gain_copy(src, first, count, stage, target):
+        dst = gains.at[pl.ds(first, count)]
+        return remote(
+            dst if src is None else src, dst, gain_sem.at[stage], gain_sem.at[3 + stage], target
+        )
+
+    gain_turn = gain_copy(own_gains, low * dev_heads, dev_heads, 0, (owner_row, y * nz + z))
+    gain_core = gain_copy(None, low * dev_heads, dev_heads, 1, other_core)
+    gain_half = gain_copy(None, half * 2 * dev_heads, 2 * dev_heads, 2, other_half)
+
+    @pl.when(x != y)
+    def _():
+        gain_turn.start()
+
+    @pl.when(x == y)
+    def _():
+        gains[pl.ds(low * dev_heads, dev_heads)] = own_gains[...]
+
+    in_sends(1)
+    @pl.loop(0, groups)
+    def _(g):
+        cols = columns(x * groups + g)
+        pltpu.make_async_copy(q_hbm.at[:, cols], qin.at[g, x, 0], own_sem).start()
+        pltpu.make_async_copy(do_hbm.at[:, cols], qin.at[g, x, 1], own_sem).start()
 
     index = lax.broadcasted_iota(jnp.int32, (1, text), 1)
     chunk_rows = NX * depth
@@ -212,14 +254,16 @@
 
     def compute(g):
         head = x * groups + g
-        gain_q = gains[head, 0:1]
-        gain_k = gains[head, 1:2]
+        gain_q = gains[g, 0:1]
+        gain_k = gains[g, 1:2]
         factor = gain_q * gain_k * (scale * LOG2E)
+        column = jnp.zeros((1, DH), F32)
         keys = kv[g, :, :, 0].reshape(text, DH)
         values = kv[g, :, :, 1].reshape(text, DH)
         for i in (1, 2, 3, 0):
             source = (x + i) % NX
-            q_low = (qin[g, source, 0].astype(F32) * inv[source] * factor).astype(BF16)
+            q_unit = qin[g, source, 0].astype(F32) * inv[source]
+            q_low = (q_unit * factor).astype(BF16)
             cot = qin[g, source, 1]
             sc = lax.dot_general(q_low, keys, nt, preferred_element_type=F32) + bias
             e = jnp.exp2(sc - jnp.max(sc, axis=-1, keepdims=True))
@@ -230,6 +274,8 @@
             dp = lax.dot_general(cot, values, nt, preferred_element_type=F32)
             ds = (e * (dp - delta)).astype(BF16)
             dq = jnp.dot(ds, keys, preferred_element_type=F32) * inv_sum * gain_k
+            column = column + jnp.sum(dq * q_unit, axis=0, keepdims=True)
+            dq = dq * (gain_q * scale)
             if i == 0:
                 att[:, columns(head)] = o_low
                 dqin[head] = dq.astype(BF16)
@@ -238,15 +284,15 @@
                 o_send[g, source, 1] = dq.astype(BF16)
                 for copy in out_copies(g, i):
                     copy.start()
+        gain_row = g // dev_heads
+        part[(gain_row % 2 * 2 + gain_row // 2) * dev_heads + g % dev_heads] = column * scale
 
     def post(g):
         settle_recv(dqin.at[pl.ds(0, NX - 1)], dq_recv.at[g])
         for xx in range(NX):
             head = xx * groups + g
             q_unit = q[:, columns(head)].astype(F32) * inv[x]
-            product = dqin[head].astype(F32) * q_unit
-            rowacc[...] += product * (gains[head, 0:1] * scale)
-            part[head] = jnp.sum(product, axis=0, keepdims=True) * scale
+            rowacc[...] += dqin[head].astype(F32) * q_unit
 
     last = nz - 1
 
@@ -286,21 +332,17 @@
                 def _():
                     z_copy(g, z + d, False).start()
 
-        @pl.when(n + 1 < groups)
-        def _():
-            in_sends(n + 1)
-
-        @pl.when(n == min(1, last - 1))
-        def _():
-            settle_recv(gains.at[pl.ds(0, (NL - 1) * dev_heads)], gain_sem.at[1])
-            row = gains.at[pl.ds(y * NL * dev_heads, NL * dev_heads)]
-            for i in range(1, ny):
-                remote(row, row, gain_sem.at[2], gain_sem.at[3], at_y(i)).start()
+        @pl.when(n + 2 < groups)
+        def _():
+            in_sends(n + 2)
 
         @pl.when(n == min(2, last - 1))
         def _():
-            if ny > 1:
-                settle_recv(gains.at[pl.ds(0, (ny - 1) * NL * dev_heads)], gain_sem.at[3])
+            @pl.when(x != y)
+            def _():
+                gain_turn.wait_recv()
+
+            gain_core.start()
             settle_recv(inv_row.at[pl.ds(0, NX - 1)], inv_sem.at[1])
             for i in range(1, NX):
                 source = (x + i) % NX
@@ -308,6 +350,15 @@
                 inv[source] = jnp.transpose(wide)[:, 0:DH]
             pltpu.make_async_copy(qin.at[:, x], qin.at[:, x], own_sem).wait()
 
+        @pl.when(n == min(3, last - 1))
+        def _():
+            gain_core.wait_recv()
+            gain_half.start()
+
+        @pl.when(n == last - 1)
+        def _():
+            gain_half.wait_recv()
+
         done = n - last
 
         @pl.when(jnp.logical_and(done >= 0, done < groups))
@@ -325,61 +376,73 @@
 
         return carry
 
-    lax.fori_loop(0, groups + last + 2, step, 0)
-
-    def final(first, count):
-        @pl.loop(first, first + count)
-        def _(head):
-            dq_unit = dqin[head].astype(F32) * (gains[head, 0:1] * scale)
-            result = inv[x] * dq_unit - q[:, columns(head)].astype(F32) * slope
-            grad[:, columns(head)] = result.astype(BF16)
-
-    for i in range(1, ny):
-        to = (y + i) % ny
-        remote(
-            part.at[pl.ds(to * NL * dev_heads, NL * dev_heads)],
+    lax.fori_loop(0, groups + last, step, 0)
+
+    span = 2 * dev_heads
+    to_core = remote(
+        part.at[pl.ds((1 - core) * span, span)], sum_c, sum_sem.at[0], sum_sem.at[1], other_core
+    )
+    to_core.start()
+    post(groups - 2)
+    to_core.wait_recv()
+    core_part[...] = part[pl.ds(core * span, span)] + sum_c[...]
+
+    def to_row(i):
+        return remote(
+            core_part,
             sum_y.at[y],
-            sum_sem.at[0],
-            sum_sem.at[1],
-            at_y(i),
-        ).start()
-    sum_y[y] = part[pl.ds(y * NL * dev_heads, NL * dev_heads)]
-    row_mean = jnp.sum(rowacc[...], axis=-1, keepdims=True) * (1.0 / (heads * DH))
-    slope = inv[x] * inv[x] * row_mean
-    final(0, heads // 4)
-    if ny > 1:
-        settle_recv(sum_y.at[pl.ds(0, ny - 1)], sum_sem.at[1])
+            sum_sem.at[2],
+            sum_sem.at[3],
+            (owner_row, (x + i) % NX * nz + z),
+        )
+
+    for i in range(1, NX):
+        to_row(i).start()
+
+    @pl.when(x != y)
+    def _():
+        to_row(0).start()
+
+    @pl.when(x == y)
+    def _():
+        sum_y[y] = core_part[...]
+
+    @pl.when(x == y)
+    def _():
+        settle_recv(sum_y.at[pl.ds(0, ny - 1)], sum_sem.at[3])
+
+    @pl.when(x != y)
+    def _():
+        settle_recv(sum_y.at[pl.ds(0, ny)], sum_sem.at[3])
+
     total = sum_y[0]
     for i in range(1, ny):
         total = total + sum_y[i]
-    row_part[...] = total
-    for i in range(1, NL):
-        to = (low + i) % NL
-        remote(
-            row_part.at[pl.ds(to * dev_heads, dev_heads)],
-            sum_l.at[low],
-            sum_sem.at[2],
-            sum_sem.at[3],
-            at_low(i),
-        ).start()
-    sum_l[low] = row_part[pl.ds(low * dev_heads, dev_heads)]
-    final(heads // 4, heads // 4)
-    settle_recv(sum_l.at[pl.ds(0, NL - 1)], sum_sem.at[3])
-    total = sum_l[0]
-    for i in range(1, NL):
-        total = total + sum_l[i]
-    sum_x[x] = total
-    for i in range(1, NX):
-        remote(sum_x.at[x], sum_x.at[x], sum_sem.at[4], sum_sem.at[5], at_x(i)).start()
-    final(heads // 2, heads // 4)
-    settle_recv(sum_x.at[pl.ds(0, NX - 1)], sum_sem.at[5])
-    total = sum_x[0]
-    for i in range(1, NX):
-        total = total + sum_x[i]
-    sum_z[z] = total
-    for i in range(1, nz):
-        remote(sum_z.at[z], sum_z.at[z], sum_sem.at[6], sum_sem.at[7], at_z(i)).start()
-    final(3 * heads // 4, heads // 4)
+    z_part[...] = total
+
+    def to_place(i):
+        to = (place + i) % places
+        return remote(
+            z_part.at[pl.ds(to // nz * dev_heads, dev_heads)],
+            sum_z.at[place],
+            sum_sem.at[4],
+            sum_sem.at[5],
+            at_place(i),
+        )
+
+    @pl.loop(0, places - 1)
+    def _(i):
+        to_place((i + places // 4) % (places - 1) + 1).start()
+
+    sum_z[place] = z_part[pl.ds(half * dev_heads, dev_heads)]
+    post(groups - 1)
+    row_mean = jnp.sum(rowacc[...], axis=-1, keepdims=True) * (1.0 / (heads * DH))
+    slope = inv[x] * inv[x] * row_mean
+
+    @pl.loop(0, heads)
+    def _(head):
+        result = inv[x] * dqin[head].astype(F32) - q[:, columns(head)].astype(F32) * slope
+        grad[:, columns(head)] = result.astype(BF16)
 
     settle_recv(att.at[:, 0 : (NX - 1) * wx], o_recv)
     settle_send(kv_send.at[0 : NX - 1], kvx_sem.at[0])
@@ -387,9 +450,18 @@
     settle_send(o_send.at[:, 0 : NX - 1, 0], o_send_sem)
     settle_send(o_send.at[:, 0 : NX - 1, 1], dq_send_sem)
     settle_send(inv_row.at[pl.ds(0, NX - 1)], inv_sem.at[0])
-    settle_send(gains.at[pl.ds(0, (NL - 1) * dev_heads)], gain_sem.at[0])
-    if ny > 1:
-        settle_send(gains.at[pl.ds(0, (ny - 1) * NL * dev_heads)], gain_sem.at[2])
+    gain_core.wait_send()
+    gain_half.wait_send()
+    to_core.wait_send()
+
+    @pl.when(x == y)
+    def _():
+        settle_send(sum_y.at[pl.ds(0, NX - 1)], sum_sem.at[2])
+
+    @pl.when(x != y)
+    def _():
+        gain_turn.wait_send()
+        settle_send(sum_y.at[pl.ds(0, NX)], sum_sem.at[2])
 
     @pl.loop(0, nz)
     def _(zz):
@@ -401,16 +473,12 @@
         def _():
             settle_send(kv.at[:, zz], zd_send.at[zz])
 
-    if ny > 1:
-        settle_send(sum_y.at[pl.ds(0, ny - 1)], sum_sem.at[0])
-    settle_send(sum_l.at[pl.ds(0, NL - 1)], sum_sem.at[2])
-    settle_send(sum_x.at[pl.ds(0, NX - 1)], sum_sem.at[4])
-    settle_recv(sum_z.at[pl.ds(0, nz - 1)], sum_sem.at[7])
+    settle_recv(sum_z.at[pl.ds(0, places - 1)], sum_sem.at[5])
     total = sum_z[0]
-    for i in range(1, nz):
+    for i in range(1, places):
         total = total + sum_z[i]
     gg_ref[...] = total
-    settle_send(sum_z.at[pl.ds(0, nz - 1)], sum_sem.at[6])
+    settle_send(sum_z.at[pl.ds(0, places - 1)], sum_sem.at[4])
 
 
 def on_device(nz, nf, query_raw, out_cotangent, text_keys, text_values, text_lengths, gain_query, gain_key):
@@ -446,13 +514,14 @@
             pltpu.VMEM((NX, 1, rows), F32),
             pltpu.VMEM((NX, rows, DH), F32),
             pltpu.VMEM((rows, DH), F32),
-            pltpu.VMEM((heads, 2, DH), F32),
-            pltpu.VMEM((heads, 1, DH), F32),
-            pltpu.VMEM((NL * dev_heads, 1, DH), F32),
-            pltpu.VMEM((ny, NL * dev_heads, 1, DH), F32),
-            pltpu.VMEM((NL, dev_heads, 1, DH), F32),
-            pltpu.VMEM((NX, dev_heads, 1, DH), F32),
-            pltpu.VMEM((nz, dev_heads, 1, DH), F32),
+            pltpu.VMEM((dev_heads, 2, DH), F32),
+            pltpu.VMEM((own, 2, DH), F32),
+            pltpu.VMEM((own, 1, DH), F32),
+            pltpu.VMEM((own // 2, 1, DH), F32),
+            pltpu.VMEM((own // 2, 1, DH), F32),
+            pltpu.VMEM((ny, own // 2, 1, DH), F32),
+            pltpu.VMEM((own // 2, 1, DH), F32),
+            pltpu.VMEM((NL // 2 * nz, dev_heads, 1, DH), F32),
             dma((3,)),
             dma,
             dma((2,)),
@@ -466,8 +535,8 @@
             dma,
             dma((own,)),
             dma((2,)),
-            dma((4,)),
-            dma((8,)),
+            dma((6,)),
+            dma((6,)),
         ],
         compiler_params=pltpu.CompilerParams(
             collective_id=0, has_side_effects=True, vmem_limit_bytes=VMEM_LIMIT

time: 104 us -> 94 us (0.904)
  Pallas kernels: 98.5 us -> 88.6 us
    pallas_call x1, Pallas kernels: 98.5 us -> 88.6 us  [on_device(): pl.pallas_call(functools.partial(attention_kernel, dims), out_shape=(jax....]
where the time goes in v2:
time: 94 us; the launch traced here: 93.8 us
  Pallas kernels  88.6 us (94%)
  local copies, waits for them, and re-layouts  3.92 us (4%)
  between operations  1.3 us (1%)
    pallas_call x1, Pallas kernels, on_device(): pl.pallas_call(functools.partial(attention_kernel, dims), out_shape=(jax....  88.6 us
    unnamed x7, local copies, waits for them, and re-layouts  3.92 us

profile of v2, /device:TPU:1, one launch (start us, length us, event | category | flops | bytes accessed | tf_op | source)
XLA Modules:
  0.0 93.8 jit_solution(7150759526399630607)
XLA Ops:
  1.3 88.6 %shard_map.94 = (bf16[128,4096]{1,0:T(8,128)(2,1)}, bf16[128,4096]{1,0:T(8,128)(2,1)}, f32[2,1,128]{2,1,0:T(1,128)}) custom-call(s32[1]{0:T(128)S(6)} %copy.13.len_ref, bf16[128,4096]{1,0:T(8,128)(2,1)} %bitcast.9, bf16[128,4096]{1,0:T(8,128)(2,1)} %bitcast.10, bf16[16,4096]{1,0:T(8,128)(2,1)} %bitcast.13, bf16[16,4096]{1,0:T(8,128)(2,1)} %bitcast.14, ...), custom_call_target="tpu_custom_call" | custom-call | tf_op jit(solution)/shard_map/pallas_call | solution.py:496
  89.9 0.0 copy-start
  89.9 2.4 %copy.14 = bf16[1,128,4096]{2,1,0:T(8,128)(2,1)} copy(bf16[1,128,4096]{2,1,0:T(8,128)(2,1)} %bitcast.12) | data formatting | bytes 2097152
  92.3 0.0 copy-done
  92.3 0.0 copy-start.1
  92.3 1.0 %copy.15 = bf16[1,128,4096]{2,1,0:T(8,128)(2,1)} copy(bf16[1,128,4096]{2,1,0:T(8,128)(2,1)S(1)} %bitcast.11) | data formatting | bytes 2097152
  93.2 0.0 copy-done.1
  93.2 0.6 copy.16
Async XLA Ops:
  89.9 2.4 %copy-start = (bf16[128,4096]{1,0:T(8,128)(2,1)S(1)}, bf16[128,4096]{1,0:T(8,128)(2,1)}, u32[]{:S(2)}) copy-start(bf16[128,4096]{1,0:T(8,128)(2,1)} %get-tuple-element.7) | copy-start | bytes 3145732
  92.3 1.0 %copy-start.1 = (f32[2,1,128]{2,1,0:T(1,128)S(1)}, f32[2,1,128]{2,1,0:T(1,128)}, u32[]{:S(2)}) copy-start(f32[2,1,128]{2,1,0:T(1,128)} %get-tuple-element.8) | copy-start | bytes 3076

commit v3 on v2

--- a/solution.py
+++ b/solution.py
@@ -11,6 +11,7 @@
 DH = 128
 NX = 4
 NL = 4
+AHEAD = 2
 EPS = 1e-6
 LOG2E = 1.4426950408889634
 MASKED = -1e30
@@ -296,20 +297,26 @@
 
     last = nz - 1
 
+    def own_sends(g):
+        @pl.when(z < last)
+        def _():
+            z_copy(g, z, True).start()
+
+        @pl.when(z > 0)
+        def _():
+            z_copy(g, z, False).start()
+
     def step(n, carry):
         @pl.when(n == 0)
         def _():
             settle_recv(kv.at[:, z, 0 : NX - 1], kvx_sem.at[1])
 
-        @pl.when(n < groups)
-        def _():
-            @pl.when(z < last)
-            def _():
-                z_copy(n, z, True).start()
-
-            @pl.when(z > 0)
-            def _():
-                z_copy(n, z, False).start()
+            for g in range(AHEAD):
+                own_sends(g)
+
+        @pl.when(n + AHEAD < groups)
+        def _():
+            own_sends(n + AHEAD)
 
         @pl.loop(1, nz)
         def _(d):
@@ -368,12 +375,6 @@
                 settle_recv(qin.at[done, source], in_recv.at[done, source])
             compute(done)
 
-        returned = done - 2
-
-        @pl.when(jnp.logical_and(returned >= 0, returned < groups))
-        def _():
-            post(returned)
-
         return carry
 
     lax.fori_loop(0, groups + last, step, 0)
@@ -383,7 +384,6 @@
         part.at[pl.ds((1 - core) * span, span)], sum_c, sum_sem.at[0], sum_sem.at[1], other_core
     )
     to_core.start()
-    post(groups - 2)
     to_core.wait_recv()
     core_part[...] = part[pl.ds(core * span, span)] + sum_c[...]
 
@@ -406,6 +406,10 @@
     @pl.when(x == y)
     def _():
         sum_y[y] = core_part[...]
+
+    @pl.loop(0, groups - 2)
+    def _(g):
+        post(g)
 
     @pl.when(x == y)
     def _():
@@ -435,6 +439,7 @@
         to_place((i + places // 4) % (places - 1) + 1).start()
 
     sum_z[place] = z_part[pl.ds(half * dev_heads, dev_heads)]
+    post(groups - 2)
     post(groups - 1)
     row_mean = jnp.sum(rowacc[...], axis=-1, keepdims=True) * (1.0 / (heads * DH))
     slope = inv[x] * inv[x] * row_mean

time: 94 us -> 92.2 us (0.981)
  Pallas kernels: 88.6 us -> 86.8 us
    pallas_call x1, Pallas kernels: 88.6 us -> 86.8 us  [on_device(): pl.pallas_call(functools.partial(attention_kernel, dims), out_shape=(jax....]
where the time goes in v3:
time: 92.2 us; the launch traced here: 92 us
  Pallas kernels  86.8 us (94%)
  local copies, waits for them, and re-layouts  3.92 us (4%)
  between operations  1.3 us (1%)
    pallas_call x1, Pallas kernels, on_device(): pl.pallas_call(functools.partial(attention_kernel, dims), out_shape=(jax....  86.8 us
    unnamed x7, local copies, waits for them, and re-layouts  3.92 us

profile of v3, /device:TPU:1, one launch (start us, length us, event | category | flops | bytes accessed | tf_op | source)
XLA Modules:
  0.0 92.0 jit_solution(1212670459158199004)
XLA Ops:
  1.3 86.8 %shard_map.94 = (bf16[128,4096]{1,0:T(8,128)(2,1)}, bf16[128,4096]{1,0:T(8,128)(2,1)}, f32[2,1,128]{2,1,0:T(1,128)}) custom-call(s32[1]{0:T(128)S(6)} %copy.13.len_ref, bf16[128,4096]{1,0:T(8,128)(2,1)} %bitcast.9, bf16[128,4096]{1,0:T(8,128)(2,1)} %bitcast.10, bf16[16,4096]{1,0:T(8,128)(2,1)} %bitcast.13, bf16[16,4096]{1,0:T(8,128)(2,1)} %bitcast.14, ...), custom_call_target="tpu_custom_call" | custom-call | tf_op jit(solution)/shard_map/pallas_call | solution.py:501
  88.0 0.0 copy-start
  88.1 2.4 %copy.14 = bf16[1,128,4096]{2,1,0:T(8,128)(2,1)} copy(bf16[1,128,4096]{2,1,0:T(8,128)(2,1)} %bitcast.12) | data formatting | bytes 2097152
  90.4 0.0 copy-done
  90.4 0.0 copy-start.1
  90.4 1.0 %copy.15 = bf16[1,128,4096]{2,1,0:T(8,128)(2,1)} copy(bf16[1,128,4096]{2,1,0:T(8,128)(2,1)S(1)} %bitcast.11) | data formatting | bytes 2097152
  91.4 0.0 copy-done.1
  91.4 0.6 copy.16
Async XLA Ops:
  88.0 2.4 %copy-start = (bf16[128,4096]{1,0:T(8,128)(2,1)S(1)}, bf16[128,4096]{1,0:T(8,128)(2,1)}, u32[]{:S(2)}) copy-start(bf16[128,4096]{1,0:T(8,128)(2,1)} %get-tuple-element.7) | copy-start | bytes 3145732
  90.4 1.0 %copy-start.1 = (f32[2,1,128]{2,1,0:T(1,128)S(1)}, f32[2,1,128]{2,1,0:T(1,128)}, u32[]{:S(2)}) copy-start(f32[2,1,128]{2,1,0:T(1,128)} %get-tuple-element.8) | copy-start | bytes 3076

commit v4 on v3

--- a/solution.py
+++ b/solution.py
@@ -11,7 +11,7 @@
 DH = 128
 NX = 4
 NL = 4
-AHEAD = 2
+AHEAD = 4
 EPS = 1e-6
 LOG2E = 1.4426950408889634
 MASKED = -1e30

time: 92.2 us -> 91.6 us (level)
  no operation moved by 1% of the time
where the time goes in v4:
time: 91.6 us; the launch traced here: 91.4 us
  Pallas kernels  86.2 us (94%)
  local copies, waits for them, and re-layouts  3.92 us (4%)
  between operations  1.3 us (1%)
    pallas_call x1, Pallas kernels, on_device(): pl.pallas_call(functools.partial(attention_kernel, dims), out_shape=(jax....  86.2 us
    unnamed x7, local copies, waits for them, and re-layouts  3.92 us

profile of v4, /device:TPU:1, one launch (start us, length us, event | category | flops | bytes accessed | tf_op | source)
XLA Modules:
  0.0 91.4 jit_solution(6241371316884947333)
XLA Ops:
  1.3 86.2 %shard_map.94 = (bf16[128,4096]{1,0:T(8,128)(2,1)}, bf16[128,4096]{1,0:T(8,128)(2,1)}, f32[2,1,128]{2,1,0:T(1,128)}) custom-call(s32[1]{0:T(128)S(6)} %copy.13.len_ref, bf16[128,4096]{1,0:T(8,128)(2,1)} %bitcast.9, bf16[128,4096]{1,0:T(8,128)(2,1)} %bitcast.10, bf16[16,4096]{1,0:T(8,128)(2,1)} %bitcast.13, bf16[16,4096]{1,0:T(8,128)(2,1)} %bitcast.14, ...), custom_call_target="tpu_custom_call" | custom-call | tf_op jit(solution)/shard_map/pallas_call | solution.py:501
  87.4 0.0 copy-start
  87.5 2.4 %copy.14 = bf16[1,128,4096]{2,1,0:T(8,128)(2,1)} copy(bf16[1,128,4096]{2,1,0:T(8,128)(2,1)} %bitcast.12) | data formatting | bytes 2097152
  89.8 0.0 copy-done
  89.8 0.0 copy-start.1
  89.8 1.0 %copy.15 = bf16[1,128,4096]{2,1,0:T(8,128)(2,1)} copy(bf16[1,128,4096]{2,1,0:T(8,128)(2,1)S(1)} %bitcast.11) | data formatting | bytes 2097152
  90.8 0.0 copy-done.1
  90.8 0.6 copy.16
Async XLA Ops:
  87.4 2.4 %copy-start = (bf16[128,4096]{1,0:T(8,128)(2,1)S(1)}, bf16[128,4096]{1,0:T(8,128)(2,1)}, u32[]{:S(2)}) copy-start(bf16[128,4096]{1,0:T(8,128)(2,1)} %get-tuple-element.7) | copy-start | bytes 3145732
  89.8 1.0 %copy-start.1 = (f32[2,1,128]{2,1,0:T(1,128)S(1)}, f32[2,1,128]{2,1,0:T(1,128)}, u32[]{:S(2)}) copy-start(f32[2,1,128]{2,1,0:T(1,128)} %get-tuple-element.8) | copy-start | bytes 3076
